TPU v7x, 32 devices: a whole 2x2x4 slice. The times are simulated.
32 devices in a mesh: seq: 4 (over y, core), dp: 8 (over z, x).
Axes of the slice: x: 2, y: 2, z: 4, core: 2. Of those that a mesh axis runs over, the one named last changes fastest.
Arguments:
- tokens: bfloat16 [8, 1024, 1280], P('dp', 'seq'), may hold values from -6 to 6
- lengths: int32 [8, 8], P('dp'), may hold values from 1 to 1016, as said below
- norm_attn: bfloat16 [1280], P(('seq', 'dp')), may hold values from 0.5 to 1.5
- norm_mlp: bfloat16 [1280], P(('seq', 'dp')), may hold values from 0.5 to 1.5
- query_scale: bfloat16 [1280], P(('seq', 'dp')), may hold values from -1 to 1.5
- query_proj: bfloat16 [1280, 1280], P(('seq', 'dp')), may hold values from -0.15625 to 0.15625
- key_proj: bfloat16 [1280, 1280], P(('seq', 'dp')), may hold values from -0.15625 to 0.15625
- value_proj: bfloat16 [1280, 1280], P(('seq', 'dp')), may hold values from -0.15625 to 0.15625
- output_proj: bfloat16 [1280, 1280], P(('seq', 'dp')), may hold values from -1.25 to 1.25
- gate_proj: bfloat16 [1280, 1280], P(('seq', 'dp')), may hold values from -0.15625 to 0.15625
- up_proj: bfloat16 [1280, 1280], P(('seq', 'dp')), may hold values from -0.15625 to 0.15625
- down_proj: bfloat16 [1280, 1280], P(('seq', 'dp')), may hold values from -0.15625 to 0.15625
- cotangent: bfloat16 [8, 1024, 1280], P('dp', 'seq'), may hold values from -6 to 6
Outputs:
- block_out: bfloat16 [8, 1024, 1280], P('dp', 'seq')
- grad_tokens: float32 [8, 1024, 1280], P('dp', 'seq')
- grad_norm_attn: float32 [1280], P(('seq', 'dp'))
- grad_norm_mlp: float32 [1280], P(('seq', 'dp'))
- grad_query_scale: float32 [1280], P(('seq', 'dp'))
- grad_query_proj: float32 [1280, 1280], P(('seq', 'dp'))
- grad_key_proj: float32 [1280, 1280], P(('seq', 'dp'))
- grad_value_proj: float32 [1280, 1280], P(('seq', 'dp'))
- grad_output_proj: float32 [1280, 1280], P(('seq', 'dp'))
- grad_gate_proj: float32 [1280, 1280], P(('seq', 'dp'))
- grad_up_proj: float32 [1280, 1280], P(('seq', 'dp'))
- grad_down_proj: float32 [1280, 1280], P(('seq', 'dp'))
Inputs may be any that keep to these rules, and one draw needn't show every extreme that they name: Each row holds the lengths of 8 documents packed in order into one sequence of 1024 positions; their sum is less than 1024, and the positions past it are padding. In every row one document starts within the first 256 positions and ends within the last 256.
All inputs are finite; a program needn't handle non-finite values.
Results may differ from a plain program's by a relative error of at most 0.015.
Values may be sent and summed in bfloat16 or wider, within the bound.
No kernel may reach another device: no remote copies, remote signals or barrier semaphores. Data moves between devices by JAX's collectives and lax.ppermute only.
A program may use at most 256 MiB of HBM per device.

v0:
```python
import jax
import jax.numpy as jnp
from jax import lax
from jax.sharding import PartitionSpec as P

H = 16
HD = 80


EPSILON = 1e-06
R_SOFTPLUS = 1.442695041
MASKED = -1e30
TAIL_WIDTH = 128


def norm_rows(values, gain):
    inverse = lax.rsqrt(jnp.mean(values * values, axis=-1, keepdims=True) + EPSILON)
    return (values * inverse * gain, inverse)


def norm_back(values, inverse, gain, upstream):
    scaled = upstream * gain
    return inverse * scaled - values * inverse**3 * jnp.mean(
        values * scaled, axis=-1, keepdims=True
    )


def segment_rows(lengths_row, length):
    doc_ends = jnp.cumsum(lengths_row)
    places = jnp.arange(length, dtype=jnp.int32)
    segment = jnp.sum((places[:, None] >= doc_ends[None, :]).astype(jnp.int32), axis=1)
    return (segment, places < doc_ends[-1])


def outer_sum(left, right):
    return lax.dot_general(
        left, right, (((0,), (0,)), ((), ())), preferred_element_type=jnp.float32
    )


def times_transpose(left, right):
    return lax.dot_general(
        left, right, (((1,), (1,)), ((), ())), preferred_element_type=jnp.float32
    )


def row_terms(vectors, pairs):
    blocks = [outer_sum(left, right) for left, right in pairs]
    tail = jnp.stack([vector for vector in vectors], axis=1)
    tail = jnp.pad(tail, ((0, 0), (0, TAIL_WIDTH - len(vectors))))
    return jnp.concatenate(blocks + [tail], axis=1)


def split_terms(summed, vector_count, pair_count, width):
    matrices = [summed[:, index * width : (index + 1) * width] for index in range(pair_count)]
    base = pair_count * width
    vectors = [summed[:, base + index] for index in range(vector_count)]
    return (vectors, matrices)


def to_heads(matrix):
    return matrix.reshape(matrix.shape[0], H, HD).transpose(1, 0, 2)


def from_heads(stacked):
    return stacked.transpose(1, 0, 2).reshape(stacked.shape[1], H * HD)


def masked_scores(query_rows, key_block, row_ids, row_segments, key_start, key_segments):
    raw_scores = jnp.einsum("qd,kd->qk", query_rows, key_block, preferred_element_type=jnp.float32)
    col_ids = key_start + jnp.arange(key_block.shape[0], dtype=jnp.int32)
    allowed = (col_ids[None, :] <= row_ids[:, None]) & (
        key_segments[None, :] == row_segments[:, None]
    )
    return jnp.where(allowed, raw_scores, MASKED)


def head_forward(query_head, key_head, value_head, seg_query, seg_keys, first_row):
    row_count, head_width = query_head.shape
    length = key_head.shape[0]
    query_size = min(512, row_count)
    key_size = min(512, length)
    key_starts = jnp.arange(length // key_size, dtype=jnp.int32) * key_size
    row_starts = first_row + jnp.arange(row_count // query_size, dtype=jnp.int32) * query_size

    def query_block(block_item):
        query_rows, row_segments, row_start = block_item
        row_ids = row_start + jnp.arange(query_size, dtype=jnp.int32)

        def key_scores(key_start):

            def compute():
                key_block = lax.dynamic_slice_in_dim(key_head, key_start, key_size, 0)
                key_segments = lax.dynamic_slice_in_dim(seg_keys, key_start, key_size, 0)
                return masked_scores(
                    query_rows, key_block, row_ids, row_segments, key_start, key_segments
                )

            return compute()

        scores = lax.map(key_scores, key_starts)
        row_max = jnp.max(scores, axis=(0, 2))
        exp_scores = jnp.exp(scores - row_max[None, :, None])
        row_total = jnp.sum(exp_scores, axis=(0, 2))
        weights_p = (exp_scores / row_total[None, :, None]).astype(jnp.bfloat16)

        def add_values(acc_rows, key_item):
            block_weights, key_start = key_item

            def compute():
                value_block = lax.dynamic_slice_in_dim(value_head, key_start, key_size, 0)
                return acc_rows + jnp.dot(
                    block_weights, value_block, preferred_element_type=jnp.float32
                )

            return (compute(), None)

        mixed_rows, unused = lax.scan(
            add_values, jnp.zeros((query_size, head_width), jnp.float32), (weights_p, key_starts)
        )
        return (mixed_rows, row_max, row_total)

    return lax.map(
        query_block,
        (
            query_head.reshape(-1, query_size, head_width),
            seg_query.reshape(-1, query_size),
            row_starts,
        ),
    )


def head_backward(
    query_head,
    key_head,
    value_head,
    grad_head,
    out_head,
    row_maxes,
    row_totals,
    seg_query,
    seg_keys,
    first_row,
):
    row_count, head_width = query_head.shape
    length = key_head.shape[0]
    query_size = min(512, row_count)
    key_size = min(512, length)
    key_starts = jnp.arange(length // key_size, dtype=jnp.int32) * key_size
    row_starts = first_row + jnp.arange(row_count // query_size, dtype=jnp.int32) * query_size

    def query_block(key_grads, block_item):
        query_rows, grad_rows, out_rows, row_max, row_total, row_segments, row_start = block_item
        row_delta = jnp.sum(grad_rows.astype(jnp.float32) * out_rows, axis=1)
        row_ids = row_start + jnp.arange(query_size, dtype=jnp.int32)

        def key_block_step(grad_query, key_start):
            key_block = lax.dynamic_slice_in_dim(key_head, key_start, key_size, 0)
            value_block = lax.dynamic_slice_in_dim(value_head, key_start, key_size, 0)
            key_segments = lax.dynamic_slice_in_dim(seg_keys, key_start, key_size, 0)

            def compute():
                scores = masked_scores(
                    query_rows, key_block, row_ids, row_segments, key_start, key_segments
                )
                probs_f = jnp.exp(scores - row_max[:, None]) / row_total[:, None]
                grad_probs = jnp.einsum(
                    "qd,kd->qk", grad_rows, value_block, preferred_element_type=jnp.float32
                )
                grad_scores = (probs_f * (grad_probs - row_delta[:, None])).astype(jnp.bfloat16)
                new_query = grad_query + jnp.dot(
                    grad_scores, key_block, preferred_element_type=jnp.float32
                )
                grad_key_part = jnp.einsum(
                    "qk,qd->kd", grad_scores, query_rows, preferred_element_type=jnp.float32
                )
                grad_value_part = jnp.einsum(
                    "qk,qd->kd",
                    probs_f.astype(jnp.bfloat16),
                    grad_rows,
                    preferred_element_type=jnp.float32,
                )
                return (new_query, grad_key_part, grad_value_part)

            grad_query, grad_key_part, grad_value_part = compute()
            return (grad_query, (grad_key_part, grad_value_part))

        grad_query, (key_parts, value_parts) = lax.scan(
            key_block_step, jnp.zeros((query_size, head_width), jnp.float32), key_starts
        )
        return (
            (
                key_grads[0] + key_parts.reshape(length, head_width),
                key_grads[1] + value_parts.reshape(length, head_width),
            ),
            grad_query,
        )

    zero_keys = jnp.zeros((length, head_width), jnp.float32)
    blocks = (
        query_head.reshape(-1, query_size, head_width),
        grad_head.reshape(-1, query_size, head_width),
        out_head.reshape(-1, query_size, head_width),
        row_maxes,
        row_totals,
        seg_query.reshape(-1, query_size),
        row_starts,
    )
    (grad_keys, grad_values), grad_queries = lax.scan(query_block, (zero_keys, zero_keys), blocks)
    return (grad_queries.reshape(row_count, head_width), grad_keys, grad_values)


def local(
    tokens,
    lengths,
    norm_attn,
    norm_mlp,
    query_scale,
    query_proj,
    key_proj,
    value_proj,
    output_proj,
    gate_proj,
    up_proj,
    down_proj,
    cotangent,
):
    inputs = tokens[0].astype(jnp.float32)
    row_count = inputs.shape[0]
    length = row_count * lax.axis_size("seq")
    first_row = lax.axis_index("seq") * row_count
    seg_keys, valid_keys = segment_rows(lengths[0], length)
    seg_query = lax.dynamic_slice_in_dim(seg_keys, first_row, row_count, 0)
    valid_query = lax.dynamic_slice_in_dim(valid_keys, first_row, row_count, 0)
    width = H * HD
    gathered = (
        lax.all_gather(norm_attn, ("seq", "dp"), axis=0, tiled=True),
        lax.all_gather(norm_mlp, ("seq", "dp"), axis=0, tiled=True),
        lax.all_gather(query_scale, ("seq", "dp"), axis=0, tiled=True),
        lax.all_gather(query_proj, ("seq", "dp"), axis=0, tiled=True),
        lax.all_gather(key_proj, ("seq", "dp"), axis=0, tiled=True),
        lax.all_gather(value_proj, ("seq", "dp"), axis=0, tiled=True),
        lax.all_gather(output_proj, ("seq", "dp"), axis=0, tiled=True),
        lax.all_gather(gate_proj, ("seq", "dp"), axis=0, tiled=True),
        lax.all_gather(up_proj, ("seq", "dp"), axis=0, tiled=True),
        lax.all_gather(down_proj, ("seq", "dp"), axis=0, tiled=True),
    )
    gain_a = gathered[0].astype(jnp.float32)
    gain_m = gathered[1].astype(jnp.float32)
    scale_logit = gathered[2].astype(jnp.float32)
    proj_q, proj_k, proj_v, proj_o, proj_g, proj_u, proj_d = gathered[3:]
    scale_vec = R_SOFTPLUS * HD ** (-0.5) * jax.nn.softplus(scale_logit)
    normed_f, inverse_a = norm_rows(inputs, gain_a)
    normed = normed_f.astype(jnp.bfloat16)
    q_raw = jnp.dot(normed, proj_q, preferred_element_type=jnp.float32)
    queries = (q_raw * scale_vec).astype(jnp.bfloat16)
    key_rows = jnp.dot(normed, proj_k, preferred_element_type=jnp.float32).astype(jnp.bfloat16)
    value_rows = jnp.dot(normed, proj_v, preferred_element_type=jnp.float32).astype(jnp.bfloat16)
    keys_all, values_all = (
        lax.all_gather(key_rows, "seq", axis=0, tiled=True),
        lax.all_gather(value_rows, "seq", axis=0, tiled=True),
    )
    heads_q = to_heads(queries)
    heads_k = to_heads(keys_all)
    heads_v = to_heads(values_all)

    def forward_head(head_item):
        return head_forward(
            head_item[0], head_item[1], head_item[2], seg_query, seg_keys, first_row
        )

    head_out, row_maxes, row_totals = lax.map(forward_head, (heads_q, heads_k, heads_v))
    heads_out = head_out.reshape(H, row_count, HD)
    attended_f = from_heads(heads_out)
    attended = attended_f.astype(jnp.bfloat16)
    hidden1 = inputs + jnp.dot(attended, proj_o, preferred_element_type=jnp.float32)
    normed_m_f, inverse_m = norm_rows(hidden1, gain_m)
    normed_m = normed_m_f.astype(jnp.bfloat16)
    gate_pre = jnp.dot(normed_m, proj_g, preferred_element_type=jnp.float32)
    up_pre = jnp.dot(normed_m, proj_u, preferred_element_type=jnp.float32)
    sigmoid_gate = jax.nn.sigmoid(gate_pre)
    hidden = (gate_pre * sigmoid_gate * up_pre).astype(jnp.bfloat16)
    block_out = hidden1 + jnp.dot(hidden, proj_d, preferred_element_type=jnp.float32)
    upstream = cotangent[0].astype(jnp.float32) * valid_query[:, None].astype(jnp.float32)
    matrices = (
        lax.all_gather(query_proj, ("seq", "dp"), axis=0, tiled=True),
        lax.all_gather(key_proj, ("seq", "dp"), axis=0, tiled=True),
        lax.all_gather(value_proj, ("seq", "dp"), axis=0, tiled=True),
        lax.all_gather(output_proj, ("seq", "dp"), axis=0, tiled=True),
        lax.all_gather(gate_proj, ("seq", "dp"), axis=0, tiled=True),
        lax.all_gather(up_proj, ("seq", "dp"), axis=0, tiled=True),
        lax.all_gather(down_proj, ("seq", "dp"), axis=0, tiled=True),
    )
    proj_q, proj_k, proj_v, proj_o, proj_g, proj_u, proj_d = matrices
    upstream_b = upstream.astype(jnp.bfloat16)
    grad_hidden = times_transpose(upstream_b, proj_d)
    grad_up = (grad_hidden * gate_pre * sigmoid_gate).astype(jnp.bfloat16)
    grad_gate = (
        grad_hidden * up_pre * sigmoid_gate * (1.0 + gate_pre * (1.0 - sigmoid_gate))
    ).astype(jnp.bfloat16)
    grad_normed_m = times_transpose(grad_gate, proj_g) + times_transpose(grad_up, proj_u)
    grad_gain_m = jnp.sum(grad_normed_m * hidden1 * inverse_m, axis=0)
    grad_hidden1 = upstream + norm_back(hidden1, inverse_m, gain_m, grad_normed_m)
    grad_hidden1_b = grad_hidden1.astype(jnp.bfloat16)
    grad_attended = times_transpose(grad_hidden1_b, proj_o).astype(jnp.bfloat16)

    def backward_head(head_item):
        return head_backward(
            head_item[0],
            head_item[1],
            head_item[2],
            head_item[3],
            head_item[4],
            head_item[5],
            head_item[6],
            seg_query,
            seg_keys,
            first_row,
        )

    head_dq, head_dk, head_dv = lax.map(
        backward_head,
        (heads_q, heads_k, heads_v, to_heads(grad_attended), heads_out, row_maxes, row_totals),
    )
    grad_queries = from_heads(head_dq)
    key_terms = from_heads(head_dk)
    value_terms = from_heads(head_dv)
    grad_keys_f, grad_values_f = (
        lax.psum_scatter(
            key_terms.astype(jnp.bfloat16), "seq", scatter_dimension=0, tiled=True
        ).astype(jnp.float32),
        lax.psum_scatter(
            value_terms.astype(jnp.bfloat16), "seq", scatter_dimension=0, tiled=True
        ).astype(jnp.float32),
    )
    grad_keys = grad_keys_f.astype(jnp.bfloat16)
    grad_values = grad_values_f.astype(jnp.bfloat16)
    grad_q_raw = (grad_queries * scale_vec).astype(jnp.bfloat16)
    grad_scale = (
        jnp.sum(q_raw * grad_queries, axis=0)
        * R_SOFTPLUS
        * HD ** (-0.5)
        * jax.nn.sigmoid(scale_logit)
    )
    grad_normed = (
        times_transpose(grad_q_raw, proj_q)
        + times_transpose(grad_keys, proj_k)
        + times_transpose(grad_values, proj_v)
    )
    grad_gain_a = jnp.sum(grad_normed * inputs * inverse_a, axis=0)
    grad_inputs = grad_hidden1 + norm_back(inputs, inverse_a, gain_a, grad_normed)
    all_flat = lax.psum_scatter(
        row_terms(
            [grad_gain_a, grad_gain_m, grad_scale],
            [
                (normed, grad_q_raw),
                (normed, grad_keys),
                (normed, grad_values),
                (attended, grad_hidden1_b),
                (normed_m, grad_gate),
                (normed_m, grad_up),
                (hidden, upstream_b),
            ],
        ),
        ("seq", "dp"),
        scatter_dimension=0,
        tiled=True,
    )
    all_vectors, all_matrices = split_terms(all_flat, 3, 7, width)
    summed = tuple(all_vectors) + tuple(all_matrices)
    return (
        block_out.astype(jnp.bfloat16)[None],
        grad_inputs[None],
        summed[0],
        summed[1],
        summed[2],
        summed[3],
        summed[4],
        summed[5],
        summed[6],
        summed[7],
        summed[8],
        summed[9],
    )


def solution(mesh):
    return jax.shard_map(
        local,
        mesh=mesh,
        in_specs=(
            P("dp", "seq", None),
            P("dp", None),
            P(("seq", "dp")),
            P(("seq", "dp")),
            P(("seq", "dp")),
            P(("seq", "dp"), None),
            P(("seq", "dp"), None),
            P(("seq", "dp"), None),
            P(("seq", "dp"), None),
            P(("seq", "dp"), None),
            P(("seq", "dp"), None),
            P(("seq", "dp"), None),
            P("dp", "seq", None),
        ),
        out_specs=(
            P("dp", "seq", None),
            P("dp", "seq", None),
            P(("seq", "dp")),
            P(("seq", "dp")),
            P(("seq", "dp")),
            P(("seq", "dp"), None),
            P(("seq", "dp"), None),
            P(("seq", "dp"), None),
            P(("seq", "dp"), None),
            P(("seq", "dp"), None),
            P(("seq", "dp"), None),
            P(("seq", "dp"), None),
        ),
        check_vma=False,
    )
```

profile of v0, /device:TPU:0, one launch (start us, length us, event | category | flops | bytes accessed | tf_op | source)
XLA Modules:
  0.0 1591.5 jit_solution(11874936422920877687)
XLA Ops:
  12.0 42.2 %all-reduce.5 = (bf16[1280]{0:T(1024)(128)(2,1)S(1)}, bf16[1280]{0:T(1024)(128)(2,1)S(1)}, bf16[1280]{0:T(1024)(128)(2,1)S(1)}) all-reduce(bf16[1280]{0:T(1024)(128)(2,1)S(1)} %dynamic-update-slice, bf16[1280]{0:T(1024)(128)(2,1)S(1)} %dynamic-update-slice.1, ...), channel_id=1, replica_groups=mesh['seq'=4,'dp'=8] {'seq','dp'}, use_global_device_ids=true, to_apply=%add.1 | all-reduce | flops 3840 | bytes 15360
  55.6 17.4 %all-gather.10.cloned.1.call-done = bf16[1280,1280]{1,0:T(8,128)(2,1)} async-done(((bf16[40,1280]{1,0:T(8,128)(2,1)}), bf16[1280,1280]{1,0:T(8,128)(2,1)}) %all-gather.10.cloned.1.call-update) | async-done | bytes 3276816 | tf_op jit(solution)/shard_map/all_gather | solution.py:241
  77.2 56.9 %all-gather.16.cloned.1.call-done = bf16[1280,1280]{1,0:T(8,128)(2,1)} async-done(((bf16[40,1280]{1,0:T(8,128)(2,1)}), bf16[1280,1280]{1,0:T(8,128)(2,1)}) %all-gather.16.cloned.1.call-update) | async-done | bytes 3276816 | tf_op jit(solution)/shard_map/all_gather | solution.py:242
  142.5 52.7 %all-gather.14.cloned.1.call-done = bf16[1280,1280]{1,0:T(8,128)(2,1)} async-done(((bf16[40,1280]{1,0:T(8,128)(2,1)}), bf16[1280,1280]{1,0:T(8,128)(2,1)}) %all-gather.14.cloned.1.call-update) | async-done | bytes 3276816 | tf_op jit(solution)/shard_map/all_gather | solution.py:240
  201.0 20.7 %all-gather.12.cloned.1.call-done = bf16[1024,1280]{1,0:T(8,128)(2,1)} async-done(((bf16[256,1280]{1,0:T(8,128)(2,1)}), bf16[1024,1280]{1,0:T(8,128)(2,1)}) %all-gather.12.cloned.1.call-update) | async-done | bytes 2621456 | tf_op jit(solution)/shard_map/all_gather | solution.py:260
  228.8 19.9 %all-gather.18.cloned.1.call-done = bf16[1024,1280]{1,0:T(8,128)(2,1)} async-done(((bf16[256,1280]{1,0:T(8,128)(2,1)}), bf16[1024,1280]{1,0:T(8,128)(2,1)}) %all-gather.18.cloned.1.call-update) | async-done | bytes 2621456 | tf_op jit(solution)/shard_map/all_gather | solution.py:261
  255.8 262.2 %while.90 = (s32[]{:T(128)}, f32[16,1,256,80]{2,3,1,0:T(8,128)}, f32[16,1,256]{2,1,0:T(1,128)S(1)}, f32[16,1,256]{2,1,0:T(1,128)S(1)}, bf16[16,1024,80]{2,1,0:T(...) while((s32[]{:T(128)}, f32[16,1,256,80]{2,3,1,0:T(8,128)}, ...), condition=%wide.region_10.11_spmd, body=%wide.region_3.10_spmd.sunk | while | flops 44081420 | bytes 7969489 | solution.py:272
  257.7 7.1 while.93
  274.1 7.1 while.93
  290.5 7.1 while.93
  298.7 5.6 while.94
  306.9 7.1 while.93
  323.3 7.1 while.93
  339.7 7.1 while.93
  356.1 7.1 while.93
  364.3 5.6 while.94
  372.5 7.1 while.93
  380.6 5.6 while.94
  388.9 7.1 while.93
  405.2 7.1 while.93
  421.6 7.1 while.93
  429.8 5.6 while.94
  438.0 7.1 while.93
  454.4 7.1 while.93
  470.8 7.1 while.93
  487.2 7.1 while.93
  503.6 7.1 while.93
  544.6 251.4 %while.92 = (s32[]{:T(128)}, f32[16,256,80]{1,2,0:T(8,128)}, bf16[16,1024,80]{1,2,0:T(8,128)(2,1)}, bf16[16,1024,80]{1,2,0:T(8,128)(2,1)}, bf16[16,1024,80]{2,1,...) while((s32[]{:T(128)}, f32[16,256,80]{1,2,0:T(8,128)}, ...), condition=%wide.region_17.18_spmd, body=%wide.region_13.17_spmd.sunk | while | flops 106271232 | bytes 7009914 | solution.py:321
  548.6 9.1 while.95
  564.3 9.1 while.95
  580.0 9.1 while.95
  595.7 9.1 while.95
  611.4 9.1 while.95
  627.1 9.1 while.95
  642.9 9.1 while.95
  658.6 9.1 while.95
  674.3 9.1 while.95
  690.0 9.1 while.95
  705.7 9.1 while.95
  721.5 9.1 while.95
  737.2 9.1 while.95
  752.9 9.1 while.95
  768.6 9.1 while.95
  784.3 9.1 while.95
  808.1 22.8 %reduce-scatter.4.cloned.1.call-done = bf16[256,1280]{0,1:T(8,128)(2,1)} async-done(((bf16[1024,1280]{0,1:T(8,128)(2,1)}), bf16[256,1280]{0,1:T(8,128)(2,1)}) %reduce-scatter.4.cloned.1.call-update) | async-done | bytes 655376 | tf_op jit(solution)/shard_map/reduce_scatter | solution.py:329
  835.2 33.2 %reduce-scatter.6.cloned.1.call-done = bf16[256,1280]{0,1:T(8,128)(2,1)} async-done(((bf16[1024,1280]{0,1:T(8,128)(2,1)}), bf16[256,1280]{0,1:T(8,128)(2,1)}) %reduce-scatter.6.cloned.1.call-update) | async-done | bytes 655376 | tf_op jit(solution)/shard_map/reduce_scatter | solution.py:332
  902.7 666.2 %all-reduce.8.cloned.1.call-done = f32[1280,9088]{0,1:T(8,128)} async-done(((f32[1280,9088]{0,1:T(8,128)}), f32[1280,9088]{0,1:T(8,128)}) %all-reduce.8.cloned.1.call-update) | async-done | bytes 46530576
  1568.8 6.0 fusion.80
  (1169 shorter events, 513.6 us)
Async XLA Ops:
  7.2 65.8 %all-gather.10.cloned.1.call-start = ((), (), s32[]{:S(2)}) async-start(), calls=%async_computation.2 | async-start | bytes 3379200 | tf_op jit(solution)/shard_map/all_gather | solution.py:241
  7.9 126.2 %all-gather.16.cloned.1.call-start = ((), (), s32[]{:S(2)}) async-start(), calls=%async_computation.5 | async-start | bytes 3379200 | tf_op jit(solution)/shard_map/all_gather | solution.py:242
  8.7 186.6 %all-gather.14.cloned.1.call-start = ((), (), s32[]{:S(2)}) async-start(), calls=%async_computation.4 | async-start | bytes 3379200 | tf_op jit(solution)/shard_map/all_gather | solution.py:240
  9.4 212.3 %all-gather.12.cloned.1.call-start = ((), (), s32[]{:S(2)}) async-start(), calls=%async_computation.3 | async-start | bytes 3276800 | tf_op jit(solution)/shard_map/all_gather | solution.py:260
  73.0 61.1 %copy-start = (bf16[1,256,1280]{2,1,0:T(8,128)(2,1)S(1)}, bf16[1,256,1280]{2,1,0:T(8,128)(2,1)}, u32[]{:S(2)}) copy-start(bf16[1,256,1280]{2,1,0:T(8,128)(2,1)} %param.23) | copy-start | bytes 1966084
  77.1 63.8 %copy-start.22 = (s32[1,8]{1,0:T(1,128)S(1)}, s32[1,8]{1,0:T(1,128)}, u32[]{:S(2)}) copy-start(s32[1,8]{1,0:T(1,128)} %param.24) | copy-start | bytes 100
  77.1 171.6 %all-gather.18.cloned.1.call-start = ((), (), s32[]{:S(2)}) async-start(), calls=%async_computation.6 | async-start | bytes 3276800 | tf_op jit(solution)/shard_map/all_gather | solution.py:261
  137.9 381.5 %all-gather.20.cloned.1.call-start = ((), (), s32[]{:S(2)}) async-start(), calls=%async_computation.7 | async-start | bytes 3379200 | tf_op jit(solution)/shard_map/all_gather | solution.py:243
  138.5 384.5 %all-gather.24.cloned.1.call-start = ((), (), s32[]{:S(2)}) async-start(), calls=%async_computation.9 | async-start | bytes 3379200 | tf_op jit(solution)/shard_map/all_gather | solution.py:245
  139.3 388.0 %all-gather.22.cloned.1.call-start = ((), (), s32[]{:S(2)}) async-start(), calls=%async_computation.8 | async-start | bytes 3379200 | tf_op jit(solution)/shard_map/all_gather | solution.py:244
  140.0 391.3 %all-gather.26.cloned.1.call-start = ((), (), s32[]{:S(2)}) async-start(), calls=%async_computation.10 | async-start | bytes 3379200 | tf_op jit(solution)/shard_map/all_gather | solution.py:246
  140.7 690.2 %reduce-scatter.4.cloned.1.call-start = ((), (), s32[]{:S(2)}) async-start(), calls=%async_computation.11 | async-start | bytes 3276800 | tf_op jit(solution)/shard_map/reduce_scatter | solution.py:329
  519.4 3.3 copy-start.8
  523.0 4.3 copy-start.4
  527.2 4.1 copy-start.11
  531.3 5.0 copy-start.21
  536.4 1.1 copy-start.18
  536.4 1.1 copy-start.13
  536.4 2.4 copy-start.10
  540.0 2.4 copy-start.20
  540.5 1.1 copy-start.2
  796.0 72.4 %reduce-scatter.6.cloned.1.call-start = ((), (), s32[]{:S(2)}) async-start(), calls=%async_computation.12 | async-start | bytes 3276800 | tf_op jit(solution)/shard_map/reduce_scatter | solution.py:332
  796.8 772.1 %all-reduce.8.cloned.1.call-start = ((), (), s32[]{:S(2)}) async-start(), calls=%async_computation.13 | async-start | bytes 93061120
  798.8 3.4 copy-start.1
  804.4 26.6 %copy-start.6 = (f32[256,1280]{1,0:T(8,128)S(1)}, f32[256,1280]{1,0:T(8,128)}, u32[]{:S(2)}) copy-start(f32[256,1280]{1,0:T(8,128)} %fusion.53) | copy-start | bytes 3932164
  835.2 37.9 %copy-start.7 = (bf16[256,1280]{0,1:T(8,128)(2,1)S(1)}, bf16[256,1280]{0,1:T(8,128)(2,1)}, u32[]{:S(2)}) copy-start(bf16[256,1280]{0,1:T(8,128)(2,1)} %reduce-scatter.4.cloned.1.call-done) | copy-start | bytes 1966084
  873.2 3.9 copy-start.16
  877.0 3.8 copy-start.3
  877.0 3.8 copy-start.9
  880.9 3.8 copy-start.5
  880.9 3.8 copy-start.19
  884.7 3.8 copy-start.14
  888.5 3.9 copy-start.12
  888.5 3.9 copy-start.17
  897.1 4.1 copy-start.15
Sparse Core Ops, SparseCore 0:
  10.8 62.0 all-gather.9
  75.8 58.2 all-gather.15
  136.9 58.2 all-gather.13
  197.2 24.4 all-gather.11
  223.1 25.5 all-gather.17
  251.4 59.4 all-gather.19
  313.7 58.4 all-gather.23
  375.0 58.3 all-gather.21
  436.3 58.3 all-gather.25
  796.1 34.7 reduce-scatter.3
  833.7 34.6 reduce-scatter.5
  897.2 671.5 all-reduce.7
where the time goes:
time: 1600 us; the launch traced here: 1590 us
  waiting for transfers between devices  895 us (56%)
  local copies, waits for them, and re-layouts  251 us (16%)
  loops' own time  192 us (12%)
  matrix products  129 us (8%)
  other arithmetic  65.6 us (4%)
  blocking collectives  42.2 us (3%)
    unnamed x13, waiting for transfers between devices  672 us
    another operation x16, loops' own time, query_block(): lax.scan(key_block_step, jnp.zeros((query_size, head_width), jnp.float32)...  63.9 us
    another operation x16, loops' own time, query_block(): scores = lax.map(key_scores, key_starts)  63.4 us
    another operation x16, loops' own time, query_block(): lax.scan(add_values, jnp.zeros((query_size, head_width), jnp.float32), (w...  63 us
    all_gather x1, waiting for transfers between devices, local(): lax.all_gather(value_proj, ('seq', 'dp'), axis=0, tiled=True)  56.9 us
    dynamic_slice x96, local copies, waits for them, and re-layouts, query_block(): scores = lax.map(key_scores, key_starts)  56.3 us
    all_gather x1, waiting for transfers between devices, local(): lax.all_gather(query_proj, ('seq', 'dp'), axis=0, tiled=True)  52.7 us
    unnamed x1, blocking collectives  42.2 us
  transfers between devices with their start and end apart: 12, of which 8 were waited for; matrix products, arithmetic and copies ran while one was open for 13% of the time, Pallas kernels for 0%

commit v1 on v0

v1 whole, which is shorter than its diff:
```python
import jax
import jax.numpy as jnp
from jax import lax
from jax.experimental import pallas as pl
from jax.experimental.pallas import tpu as pltpu
from jax.sharding import Mesh, PartitionSpec as P

H = 16
HD = 80
EPSILON = 1e-06
R_SOFTPLUS = 1.442695041
MASKED = -1e30
QUERY_ROWS = 256
VMEM_BYTES = 48 << 20
LONGEST_LINE = 4
F32 = jnp.float32
BF16 = jnp.bfloat16
GROUP = ("y", "z", "x")


def nn(left, right):
    return jnp.dot(left, right, preferred_element_type=F32)


def nt(left, right):
    return lax.dot_general(left, right, (((1,), (1,)), ((), ())), preferred_element_type=F32)


def tn(left, right):
    return lax.dot_general(left, right, (((0,), (0,)), ((), ())), preferred_element_type=F32)


def allowed_pairs(seg_rows, seg_keys, half, first, rows):
    total = seg_keys.shape[1]
    row_ids = lax.broadcasted_iota(jnp.int32, (rows, total), 0) + (first + half)
    col_ids = lax.broadcasted_iota(jnp.int32, (rows, total), 1)
    return (seg_rows == seg_keys) & (col_ids <= row_ids)


def forward_kernel(q_ref, k_ref, v_ref, segq_ref, segk_ref, out_ref, lse_ref):
    half, width = q_ref.shape
    for first in range(0, half, QUERY_ROWS):
        rows = slice(first, first + QUERY_ROWS)
        allowed = allowed_pairs(segq_ref[rows, :], segk_ref[...], half, first, QUERY_ROWS)
        outs, lses = [], []
        for head in range(width // HD):
            cols = slice(head * HD, (head + 1) * HD)
            scores = jnp.where(allowed, nt(q_ref[rows, cols], k_ref[:, cols]), MASKED)
            top = jnp.max(scores, axis=1, keepdims=True)
            exps = jnp.exp(scores - top)
            total = jnp.sum(exps, axis=1, keepdims=True)
            probs = (exps * (1.0 / total)).astype(BF16)
            outs.append(nn(probs, v_ref[:, cols]))
            lses.append(top + jnp.log(total))
        out_ref[rows, :] = jnp.concatenate(outs, axis=1)
        lse_ref[rows, :] = jnp.concatenate(lses, axis=1)


def backward_kernel(
    q_ref, k_ref, v_ref, go_ref, out_ref, lse_ref, segq_ref, segk_ref, dq_ref, dk_ref, dv_ref
):
    half, width = q_ref.shape
    heads = width // HD
    dks, dvs = [0.0] * heads, [0.0] * heads
    for first in range(0, half, QUERY_ROWS):
        rows = slice(first, first + QUERY_ROWS)
        allowed = allowed_pairs(segq_ref[rows, :], segk_ref[...], half, first, QUERY_ROWS)
        products = go_ref[rows, :].astype(F32) * out_ref[rows, :]
        dqs = []
        for head in range(heads):
            cols = slice(head * HD, (head + 1) * HD)
            queries, keys, values = q_ref[rows, cols], k_ref[:, cols], v_ref[:, cols]
            grads = go_ref[rows, cols]
            scores = jnp.where(allowed, nt(queries, keys), MASKED)
            probs = jnp.exp(scores - lse_ref[rows, head : head + 1])
            delta = jnp.sum(products[:, cols], axis=1, keepdims=True)
            grad_scores = (probs * (nt(grads, values) - delta)).astype(BF16)
            dqs.append(nn(grad_scores, keys))
            dks[head] = dks[head] + tn(grad_scores, queries)
            dvs[head] = dvs[head] + tn(probs.astype(BF16), grads)
        dq_ref[rows, :] = jnp.concatenate(dqs, axis=1)
    dk_ref[...] = jnp.concatenate(dks, axis=1).astype(dk_ref.dtype)
    dv_ref[...] = jnp.concatenate(dvs, axis=1).astype(dv_ref.dtype)


WHOLE = pl.BlockSpec(memory_space=pltpu.VMEM)


def attention_forward(q, k, v, segq, segk):
    return pl.pallas_call(
        forward_kernel,
        out_shape=(
            jax.ShapeDtypeStruct(q.shape, F32),
            jax.ShapeDtypeStruct((q.shape[0], q.shape[1] // HD), F32),
        ),
        in_specs=[WHOLE] * 5,
        out_specs=(WHOLE, WHOLE),
        compiler_params=pltpu.CompilerParams(vmem_limit_bytes=VMEM_BYTES),
        cost_estimate=pl.CostEstimate(flops=9000000000, bytes_accessed=8 << 20, transcendentals=4 << 20),
        name="attention_forward",
    )(q, k, v, segq, segk)


def attention_backward(q, k, v, grads, out, lse, segq, segk):
    return pl.pallas_call(
        backward_kernel,
        out_shape=(
            jax.ShapeDtypeStruct(q.shape, F32),
            jax.ShapeDtypeStruct(k.shape, BF16),
            jax.ShapeDtypeStruct(v.shape, BF16),
        ),
        in_specs=[WHOLE] * 8,
        out_specs=(WHOLE,) * 3,
        compiler_params=pltpu.CompilerParams(vmem_limit_bytes=VMEM_BYTES),
        cost_estimate=pl.CostEstimate(flops=13000000000, bytes_accessed=10 << 20, transcendentals=4 << 20),
        name="attention_backward",
    )(q, k, v, grads, out, lse, segq, segk)


def swap(value, axis):
    return lax.ppermute(value, axis, [(0, 1), (1, 0)])


def pick(pair, index):
    return jnp.where(index == 0, pair[0], pair[1])


def in_order(own, other, index, axis):
    return jnp.where(
        index == 0,
        jnp.concatenate([own, other], axis=axis),
        jnp.concatenate([other, own], axis=axis),
    )


def block_of(matrix, index, size, axis=0):
    return lax.dynamic_slice_in_dim(matrix, index * size, size, axis)


def norm_inverse(values):
    return lax.rsqrt(jnp.mean(values * values, axis=-1, keepdims=True) + EPSILON)


def norm_back(values, inverse, gain, upstream):
    scaled = upstream * gain
    return inverse * scaled - values * inverse**3 * jnp.mean(
        values * scaled, axis=-1, keepdims=True
    )


def line_scatter(parts, place, count):
    if count > LONGEST_LINE:
        return lax.psum_scatter(parts.astype(BF16), "z", scatter_dimension=0).astype(F32)
    right, left = 0.0, 0.0
    for step in range(1, count):
        ahead = lax.dynamic_index_in_dim(
            parts, jnp.minimum(place + count - step, count - 1), 0, keepdims=False
        )
        behind = lax.dynamic_index_in_dim(
            parts, jnp.maximum(place - count + step, 0), 0, keepdims=False
        )
        right = lax.ppermute(
            (ahead + right).astype(BF16), "z", [(i, i + 1) for i in range(step)]
        ).astype(F32)
        left = lax.ppermute(
            (behind + left).astype(BF16), "z", [(i, i - 1) for i in range(count - step, count)]
        ).astype(F32)
    return lax.dynamic_index_in_dim(parts, place, 0, keepdims=False) + right + left


def local(
    tokens,
    lengths,
    norm_attn,
    norm_mlp,
    query_scale,
    query_proj,
    key_proj,
    value_proj,
    output_proj,
    gate_proj,
    up_proj,
    down_proj,
    cotangent,
):
    y, c, z, x = (lax.axis_index(name) for name in ("y", "c", "z", "x"))
    line = lax.axis_size("z")
    rows = tokens.shape[1]
    share, width = query_proj.shape
    half = width // 2
    quarter = width // 4
    chip_rows = 2 * rows
    length = 4 * rows

    def halves(weight):
        split = weight.reshape(share, 2, 2, quarter)
        return [split[:, :, core].reshape(share, half) for core in range(2)]

    vector_rows = jnp.pad(
        jnp.concatenate([norm_attn, norm_mlp, query_scale])[None], ((0, 7), (0, half - 3 * share))
    )

    def by_columns(weights, tail):
        split = [halves(weight) for weight in weights]
        both = [jnp.concatenate([pair[core] for pair in split] + tail, axis=0) for core in range(2)]
        return in_order(pick(both, c), swap(pick(both, 1 - c), "c"), c, 1)

    first_message = by_columns([query_proj, key_proj, value_proj], [vector_rows])
    second_message = jnp.concatenate(
        [output_proj, down_proj, by_columns([gate_proj, up_proj], [])], axis=0
    )
    first = lax.all_gather(first_message, GROUP, axis=0, tiled=False)
    second = lax.all_gather(second_message, GROUP, axis=0, tiled=False)
    first = first.reshape((2, line, 2) + first.shape[1:])
    second = second.reshape((2, line, 2) + second.shape[1:])

    def column_weight(gathered, index):
        block = gathered[:, :, :, index * share : (index + 1) * share]
        block = block.reshape(2, line, 2, share, 2, half).transpose(0, 4, 1, 2, 3, 5)
        return block.reshape(width, half)

    def row_weight(gathered, index):
        return gathered[:, :, :, index * share : (index + 1) * share].reshape(half, width)

    proj_q, proj_k, proj_v = (column_weight(first, index) for index in range(3))
    proj_o, proj_d = (row_weight(second, index) for index in range(2))
    proj_g, proj_u = (column_weight(second, index) for index in (2, 3))
    vectors = first[:, :, :, 3 * share].reshape(2, line, 2, 2, half)[..., : 3 * share]
    vectors = vectors.reshape(2, line, 2, 2, 3, share).transpose(4, 0, 3, 1, 2, 5)
    vectors = vectors.reshape(3, width).astype(F32)
    gain_a, gain_m = vectors[0], vectors[1]
    scale_logit = lax.dynamic_index_in_dim(
        vectors[2].reshape(2, 2, quarter), c, 1, keepdims=False
    ).reshape(half)
    scale_vec = R_SOFTPLUS * HD ** (-0.5) * jax.nn.softplus(scale_logit)

    own_tokens = tokens[0]
    before = lax.ppermute(own_tokens, "y", [(0, 1)])
    chip_tokens = in_order(own_tokens, swap(own_tokens, "c"), c, 0)
    chip_before = in_order(before, swap(before, "c"), c, 0)
    doc_ends = jnp.cumsum(lengths[0])
    places = jnp.arange(length, dtype=jnp.int32)
    segment = jnp.sum((places[:, None] >= doc_ends[None, :]).astype(jnp.int32), axis=1)
    seg_here = block_of(segment, y, chip_rows)
    seg_before = jnp.where(y == 0, -1, segment[:chip_rows])
    seg_keys = jnp.concatenate([seg_before, seg_here])[None]
    valid = (y * chip_rows + jnp.arange(chip_rows, dtype=jnp.int32)) < doc_ends[-1]
    own_cotangent = cotangent[0]
    chip_cotangent = in_order(own_cotangent, swap(own_cotangent, "c"), c, 0)
    upstream_b = jnp.where(valid[:, None], chip_cotangent, 0).astype(BF16)
    upstream = block_of(upstream_b, c, rows).astype(F32)

    def reduce_rows(make):
        other = swap(make(1 - c), "c")
        return make(c) + other

    inputs = own_tokens.astype(F32)
    inverse_a = norm_inverse(inputs)
    all_tokens = jnp.concatenate([chip_before, chip_tokens], axis=0).astype(F32)
    normed = (all_tokens * norm_inverse(all_tokens) * gain_a).astype(BF16)
    normed_here = normed[chip_rows:]
    q_raw = nn(normed_here, proj_q)
    queries = (q_raw * scale_vec).astype(BF16)
    keys = nn(normed, proj_k).astype(BF16)
    values = nn(normed, proj_v).astype(BF16)
    attended_f, lse = attention_forward(queries, keys, values, seg_here[:, None], seg_keys)
    attended = attended_f.astype(BF16)
    hidden1 = inputs + reduce_rows(lambda core: nn(block_of(attended, core, rows), proj_o))
    inverse_m = norm_inverse(hidden1)
    own_normed_m = (hidden1 * inverse_m * gain_m).astype(BF16)
    normed_m = in_order(own_normed_m, swap(own_normed_m, "c"), c, 0)
    gate_pre = nn(normed_m, proj_g)
    up_pre = nn(normed_m, proj_u)
    sigmoid_gate = jax.nn.sigmoid(gate_pre)
    hidden = (gate_pre * sigmoid_gate * up_pre).astype(BF16)
    block_out = hidden1 + reduce_rows(lambda core: nn(block_of(hidden, core, rows), proj_d))

    def y_rows(left, right):
        size = left.shape[1] // 2
        other = swap(tn(block_of(left, 1 - y, size, 1), right).astype(BF16), "y")
        return tn(block_of(left, y, size, 1), right) + other.astype(F32)

    def column_grad(left, right):
        part = y_rows(left, right).reshape(2, line, 2, share, half)
        return part.transpose(1, 2, 3, 0, 4).reshape(line, 2, share, width)

    def row_grad(left, right):
        return y_rows(left, right).reshape(line, 2, share, width)

    def scatter(parts):
        part = line_scatter(jnp.concatenate(parts, axis=2), z, line)
        other = swap(pick(part, 1 - x).astype(BF16), "x").astype(F32)
        return pick(part, x) + other

    def whole_rows(part):
        split = part.reshape(part.shape[0], 2, half)
        mine, others = pick((split[:, 0], split[:, 1]), c), pick((split[:, 1], split[:, 0]), c)
        return mine, swap(others, "c")

    def whole_columns(part):
        mine, other = (side.reshape(-1, 2, 1, quarter) for side in whole_rows(part))
        return in_order(mine, other, c, 2).reshape(part.shape[0], width)

    grad_down = scatter([row_grad(hidden, upstream_b)])
    grad_hidden = nt(upstream_b, proj_d)
    grad_up = (grad_hidden * gate_pre * sigmoid_gate).astype(BF16)
    grad_gate = (
        grad_hidden * up_pre * sigmoid_gate * (1.0 + gate_pre * (1.0 - sigmoid_gate))
    ).astype(BF16)
    grad_mlp = scatter([column_grad(normed_m, grad_gate), column_grad(normed_m, grad_up)])
    grad_normed_m = reduce_rows(
        lambda core: nt(block_of(grad_gate, core, rows), proj_g)
        + nt(block_of(grad_up, core, rows), proj_u)
    )
    grad_gain_m = jnp.sum(grad_normed_m * hidden1 * inverse_m, axis=0)
    grad_hidden1 = upstream + norm_back(hidden1, inverse_m, gain_m, grad_normed_m)
    own_grad_hidden1 = grad_hidden1.astype(BF16)
    grad_hidden1_b = in_order(own_grad_hidden1, swap(own_grad_hidden1, "c"), c, 0)
    grad_output = scatter([row_grad(attended, grad_hidden1_b)])
    grad_attended = nt(grad_hidden1_b, proj_o).astype(BF16)
    grad_queries, grad_keys, grad_values = attention_backward(
        queries, keys, values, grad_attended, attended_f, lse, seg_here[:, None], seg_keys
    )
    grad_q_raw = (grad_queries * scale_vec).astype(BF16)
    grad_scale = (
        jnp.sum(q_raw * grad_queries, axis=0)
        * R_SOFTPLUS
        * HD ** (-0.5)
        * jax.nn.sigmoid(scale_logit)
    )
    grad_before = reduce_rows(
        lambda core: nt(block_of(grad_keys[:chip_rows], core, rows), proj_k)
        + nt(block_of(grad_values[:chip_rows], core, rows), proj_v)
    )
    grad_after = lax.ppermute(grad_before.astype(BF16), "y", [(1, 0)]).astype(F32)
    grad_normed = grad_after + reduce_rows(
        lambda core: nt(block_of(grad_q_raw, core, rows), proj_q)
        + nt(block_of(grad_keys[chip_rows:], core, rows), proj_k)
        + nt(block_of(grad_values[chip_rows:], core, rows), proj_v)
    )
    grad_gain_a = jnp.sum(grad_normed * inputs * inverse_a, axis=0)
    grad_inputs = grad_hidden1 + norm_back(inputs, inverse_a, gain_a, grad_normed)

    scale_rows = grad_scale.reshape(2, 1, quarter)
    scale_rows = jnp.where(
        c == 0,
        jnp.pad(scale_rows, ((0, 0), (0, 1), (0, 0))),
        jnp.pad(scale_rows, ((0, 0), (1, 0), (0, 0))),
    ).reshape(width)
    vector_terms = jnp.stack([grad_gain_a, grad_gain_m, scale_rows])
    vector_terms = vector_terms.reshape(3, 2, 2, line, 2, share).transpose(1, 3, 4, 2, 0, 5)
    vector_terms = vector_terms.reshape(2, line, 2, 1, 2, 3 * share)
    vector_terms = pick(vector_terms, y) + swap(pick(vector_terms, 1 - y), "y")
    vector_terms = jnp.pad(
        vector_terms, ((0, 0), (0, 0), (0, 7), (0, 0), (0, half - 3 * share))
    ).reshape(line, 2, 8, width)
    grad_attn = scatter(
        [
            column_grad(normed_here, grad_q_raw),
            column_grad(normed, grad_keys),
            column_grad(normed, grad_values),
            vector_terms,
        ]
    )
    vector_mine, vector_other = whole_rows(grad_attn[3 * share : 3 * share + 1])
    summed = (vector_mine + vector_other)[0, : 3 * share].reshape(3, share)
    attn_columns = whole_columns(grad_attn[: 3 * share])
    mlp_columns = whole_columns(grad_mlp)
    return (
        block_out.astype(BF16)[None],
        grad_inputs[None],
        summed[0],
        summed[1],
        summed[2],
        attn_columns[:share],
        attn_columns[share : 2 * share],
        attn_columns[2 * share :],
        grad_output,
        mlp_columns[:share],
        mlp_columns[share:],
        grad_down,
    )


def solution(mesh):
    seq, dp = mesh.devices.shape
    axes = Mesh(mesh.devices.reshape(seq // 2, 2, dp // 2, 2), ("y", "c", "z", "x"))
    batch, places, every = ("z", "x"), ("y", "c"), ("y", "c", "z", "x")
    activations = P(batch, places, None)
    vector, matrix = P(every), P(every, None)
    return jax.shard_map(
        local,
        mesh=axes,
        in_specs=(activations, P(batch, None)) + (vector,) * 3 + (matrix,) * 7 + (activations,),
        out_specs=(activations, activations) + (vector,) * 3 + (matrix,) * 7,
        check_vma=False,
    )
```

time: 1600 us -> 635 us (0.40)
  waiting for transfers between devices: 895 us -> 243 us
  loops' own time: 192 us -> 0 us
  local copies, waits for them, and re-layouts: 251 us -> 114 us
  starting transfers between devices: 0.69 us -> 86 us
  matrix products: 129 us -> 78.3 us
  blocking collectives: 42.2 us -> 0 us
  Pallas kernels: 0 us -> 35.9 us
    unnamed x13 -> x2, waiting for transfers between devices: 672 us -> 0.03 us
    another operation x50 -> x0, loops' own time: 192 us -> none  [the longest x16 63.9 us: query_block(): lax.scan(key_block_step, jnp.zeros((query_size, head_width), jnp.float32)...]
    ppermute x0 -> x53, waiting for transfers between devices: none -> 132 us  [the longest x27 73.8 us: swap(): return lax.ppermute(value, axis, [(0, 1), (1, 0)])]
    dynamic_slice x241 -> x1, local copies, waits for them, and re-layouts: 91.4 us -> 0.03 us  [local(): lax.dynamic_index_in_dim(vectors[2].reshape(2, 2, quarter), c, 1, keepdim...]
    ppermute x0 -> x53, starting transfers between devices: none -> 85.9 us  [the longest x12 43.1 us: line_scatter(): lax.ppermute((ahead + right).astype(BF16), 'z', [(i, i + 1) for i in rang...]
    squeeze x65 -> x1, local copies, waits for them, and re-layouts: 62.7 us -> 0.59 us  [local(): summed[2]]
    all_gather x9 -> x2, waiting for transfers between devices: 168 us -> 110 us  [the longest x1 59.8 us: local(): first = lax.all_gather(first_message, GROUP, axis=0, tiled=False)]
    reduce_scatter x2 -> x0, waiting for transfers between devices: 56 us -> none  [the longest x1 33.2 us: local(): lax.psum_scatter(value_terms.astype(jnp.bfloat16), 'seq', scatter_dimensi...]
  transfers between devices with their start and end apart: 12 -> 55, of which waited for: 8 -> 24; matrix products, arithmetic and copies ran while one was open for 13% -> 33% of each run, Pallas kernels for 0% -> 6%
where the time goes in v1:
time: 635 us; the launch traced here: 626 us
  waiting for transfers between devices  243 us (38%)
  local copies, waits for them, and re-layouts  114 us (18%)
  starting transfers between devices  86 us (14%)
  matrix products  78.3 us (12%)
  other arithmetic  52.5 us (8%)
  Pallas kernels  35.9 us (6%)
  between operations  16.3 us (3%)
    ppermute x27, waiting for transfers between devices, swap(): return lax.ppermute(value, axis, [(0, 1), (1, 0)])  73.8 us
    all_gather x1, waiting for transfers between devices, local(): first = lax.all_gather(first_message, GROUP, axis=0, tiled=False)  59.8 us
    all_gather x1, waiting for transfers between devices, local(): second = lax.all_gather(second_message, GROUP, axis=0, tiled=False)  50.4 us
    ppermute x12, starting transfers between devices, line_scatter(): lax.ppermute((ahead + right).astype(BF16), 'z', [(i, i + 1) for i in rang...  43.1 us
    dot_general x16, matrix products, nt(): lax.dot_general(left, right, (((1,), (1,)), ((), ())), preferred_element_...  30.3 us
    dot_general x14, matrix products, tn(): lax.dot_general(left, right, (((0,), (0,)), ((), ())), preferred_element_...  29.7 us
    ppermute x12, waiting for transfers between devices, line_scatter(): lax.ppermute((behind + left).astype(BF16), 'z', [(i, i - 1) for i in rang...  22.9 us
    pallas_call x1, Pallas kernels, attention_backward(): pl.pallas_call(backward_kernel, out_shape=(jax.ShapeDtypeStruct(q.shape,...  21.8 us
  transfers between devices with their start and end apart: 55, of which 24 were waited for; matrix products, arithmetic and copies ran while one was open for 33% of the time, Pallas kernels for 6%

profile of v1, /device:TPU:0, one launch (start us, length us, event | category | flops | bytes accessed | tf_op | source)
XLA Modules:
  0.0 625.5 jit_solution(5438271372927895177)
XLA Ops:
  19.7 4.8 collective-permute-start
  24.8 16.3 %collective-permute-done = bf16[256,1280]{1,0:T(8,128)(2,1)S(1)} collective-permute-done((bf16[256,1280]{1,0:T(8,128)(2,1)S(1)}, bf16[256,1280]{1,0:T(8,128)(2,1)S(1)}, u32[]{:S(2)}, u32[]{:S(2)}) %collective-permute-start) | collective-permute-done | bytes 655392 | tf_op jit(solution)/shard_map/ppermute | solution.py:238
  44.9 59.8 %all-gather.4.cloned.1.call-done = bf16[16,128,1280]{2,1,0:T(8,128)(2,1)} async-done(((bf16[1,128,1280]{2,1,0:T(8,128)(2,1)}), bf16[16,128,1280]{2,1,0:T(8,128)(2,1)}) %all-gather.4.cloned.1.call-update) | async-done | bytes 5242896 | tf_op jit(solution)/shard_map/all_gather | solution.py:212
  106.3 4.5 fusion.146
  110.8 4.4 reshape.613
  121.3 5.0 reshape.618
  136.8 14.1 %attention_forward.1 = (f32[512,640]{1,0:T(8,128)S(1)}, f32[512,8]{1,0:T(8,128)S(1)}) custom-call(bf16[512,640]{1,0:T(8,128)(2,1)S(1)} %get-tuple-element.97.q_ref, bf16[1024,640]{1,0:T(8,128)(2,1)S(1)} %convolution_convert_fusion.3.k_ref, bf16[1024,640]{1,0:T(8,128)(2,1)S(1)} %convolution_convert_fusion.2.v_ref, s32[512,1]{1,0:T(8,128)S(1)} %copy.133.segq_ref, ...), custom_call_target="tpu_custom_call" | custom-call | flops 8999999488 | bytes 8388608 | tf_op jit(solution)/shard_map/attention_forward/pallas_call | solution.py:90
  152.8 50.4 %all-gather.6.cloned.1.call-done = bf16[2560,1280]{1,0:T(8,128)(2,1)} async-done(((bf16[160,1280]{1,0:T(8,128)(2,1)}), bf16[2560,1280]{1,0:T(8,128)(2,1)}) %all-gather.6.cloned.1.call-update) | async-done | bytes 6553616 | tf_op jit(solution)/shard_map/all_gather | solution.py:213
  203.2 5.2 fusion.145
  224.7 4.4 reshape.625
  231.9 4.8 reshape.627
  259.6 12.6 %collective-permute-done.35 = bf16[640,640]{1,0:T(8,128)(2,1)S(1)} collective-permute-done((bf16[640,640]{1,0:T(8,128)(2,1)S(1)}, bf16[640,640]{1,0:T(8,128)(2,1)S(1)}, u32[]{:S(2)}, u32[]{:S(2)}) %collective-permute-start.35) | collective-permute-done | bytes 819232 | tf_op jit(solution)/shard_map/ppermute | solution.py:121
  275.3 3.6 reshape.642
  278.9 10.9 %collective-permute-done.36 = bf16[640,640]{1,0:T(8,128)(2,1)} collective-permute-done((bf16[640,640]{1,0:T(8,128)(2,1)}, bf16[640,640]{1,0:T(8,128)(2,1)}, u32[]{:S(2)}, u32[]{:S(2)}) %collective-permute-start.36) | collective-permute-done | bytes 819232 | tf_op jit(solution)/shard_map/ppermute | solution.py:121
  294.5 3.4 reshape.644
  299.6 7.2 %collective-permute-done.45 = bf16[320,1280]{1,0:T(8,128)(2,1)} collective-permute-done((bf16[320,1280]{1,0:T(8,128)(2,1)}, bf16[320,1280]{1,0:T(8,128)(2,1)}, u32[]{:S(2)}, u32[]{:S(2)}) %collective-permute-start.45) | collective-permute-done | bytes 819232 | tf_op jit(solution)/shard_map/ppermute | solution.py:121
  317.8 6.5 %collective-permute-done.37 = bf16[2,80,1280]{2,1,0:T(8,128)(2,1)S(1)} collective-permute-done((bf16[2,80,1280]{2,1,0:T(8,128)(2,1)S(1)}, bf16[2,80,1280]{2,1,0:T(8,128)(2,1)S(1)}, u32[]{:S(2)}, u32[]{:S(2)}) %collective-permute-start.37) | collective-permute-done | bytes 409632 | tf_op jit(solution)/shard_map/ppermute | solution.py:162
  324.3 4.4 collective-permute-start.47
  335.8 5.0 collective-permute-start.48
  340.8 3.8 multiply_reduce_fusion.1
  349.8 3.2 fusion.10
  359.1 5.4 collective-permute-start.39
  369.0 21.8 %attention_backward.1 = (f32[512,640]{1,0:T(8,128)S(1)}, bf16[1024,640]{1,0:T(8,128)(2,1)S(1)}, bf16[1024,640]{1,0:T(8,128)(2,1)S(1)}) custom-call(bf16[512,640]{1,0:T(8,128)(2,1)S(1)} %get-tuple-element.97.q_ref, bf16[1024,640]{1,0:T(8,128)(2,1)} %copy-done.1, bf16[1024,640]{1,0:T(8,128)(2,1)} %copy-done.2, ...), custom_call_target="tpu_custom_call" | custom-call | flops 12999999488 | bytes 10485760 | tf_op jit(solution)/shard_map/attention_backward/pallas_call | solution.py:105
  417.9 9.3 %collective-permute-done.42 = bf16[2,80,1280]{2,1,0:T(8,128)(2,1)S(1)} collective-permute-done((bf16[2,80,1280]{2,1,0:T(8,128)(2,1)S(1)}, bf16[2,80,1280]{2,1,0:T(8,128)(2,1)S(1)}, u32[]{:S(2)}, u32[]{:S(2)}) %collective-permute-start.42) | collective-permute-done | bytes 409632 | tf_op jit(solution)/shard_map/ppermute | solution.py:165
  431.3 3.6 convolution_convert_fusion.1
  440.6 10.7 %collective-permute-done.16 = bf16[640,640]{1,0:T(8,128)(2,1)} collective-permute-done((bf16[640,640]{1,0:T(8,128)(2,1)}, bf16[640,640]{1,0:T(8,128)(2,1)}, u32[]{:S(2)}, u32[]{:S(2)}) %collective-permute-start.16) | collective-permute-done | bytes 819232 | tf_op jit(solution)/shard_map/ppermute | solution.py:121
  455.6 13.3 %collective-permute-done.15 = bf16[640,640]{1,0:T(8,128)(2,1)} collective-permute-done((bf16[640,640]{1,0:T(8,128)(2,1)}, bf16[640,640]{1,0:T(8,128)(2,1)}, u32[]{:S(2)}, u32[]{:S(2)}) %collective-permute-start.15) | collective-permute-done | bytes 819232 | tf_op jit(solution)/shard_map/ppermute | solution.py:121
  470.3 3.6 convert_add_fusion.3
  474.1 3.1 fusion.9
  477.1 9.2 %collective-permute-done.14 = bf16[640,640]{1,0:T(8,128)(2,1)S(1)} collective-permute-done((bf16[640,640]{1,0:T(8,128)(2,1)}, bf16[640,640]{1,0:T(8,128)(2,1)S(1)}, u32[]{:S(2)}, u32[]{:S(2)}) %collective-permute-start.14) | collective-permute-done | bytes 819232 | tf_op jit(solution)/shard_map/ppermute | solution.py:121
  492.2 3.4 reshape.635
  495.6 3.9 copy.180
  499.5 3.4 reshape.633
  502.9 3.9 copy.181
  506.8 3.4 reshape.631
  510.2 3.0 convolution_add_fusion.1
  515.3 5.3 collective-permute-start.28
  522.0 3.5 fusion.18
  525.8 3.5 collective-permute-start.17
  533.2 5.3 pad_maximum_fusion
  538.5 3.0 fusion.40
  541.5 3.5 collective-permute-start.18
  555.8 5.2 collective-permute-start.19
  566.8 4.0 collective-permute-done.19
  576.5 4.3 collective-permute-start.20
  584.3 4.5 collective-permute-done.20
  588.9 13.5 %collective-permute-done.23 = bf16[2,128,1280]{2,1,0:T(8,128)(2,1)S(1)} collective-permute-done((bf16[2,128,1280]{2,1,0:T(8,128)(2,1)S(1)}, bf16[2,128,1280]{2,1,0:T(8,128)(2,1)S(1)}, u32[]{:S(2)}, u32[]{:S(2)}) %collective-permute-start.23) | collective-permute-done | bytes 655392 | tf_op jit(solution)/shard_map/ppermute | solution.py:165
  608.3 3.0 collective-permute-done.24
  (439 shorter events, 215.3 us)
Async XLA Ops:
  7.2 97.4 %all-gather.4.cloned.1.call-start = ((), (), s32[]{:S(2)}) async-start(), calls=%async_computation | async-start | bytes 5570560 | tf_op jit(solution)/shard_map/all_gather | solution.py:212
  15.0 188.2 %all-gather.6.cloned.1.call-start = ((), (), s32[]{:S(2)}) async-start(), calls=%async_computation.1 | async-start | bytes 6963200 | tf_op jit(solution)/shard_map/all_gather | solution.py:213
  19.7 21.4 %collective-permute-start = (bf16[256,1280]{1,0:T(8,128)(2,1)S(1)}, bf16[256,1280]{1,0:T(8,128)(2,1)S(1)}, u32[]{:S(2)}, u32[]{:S(2)}) collective-permute-start(bf16[256,1280]{1,0:T(8,128)(2,1)S(1)} %bitcast.258), channel_id=1, source_target_pairs={{0,16},{1,17},{2,18},{3,19},{4,20},{5,21},{6,22},{7,23},{8,24},{9,... | collective-permute-start | bytes 1966088 | tf_op jit(solution)/shard_map/ppermute | solution.py:238
  24.5 17.0 %collective-permute-start.2 = (bf16[256,1280]{1,0:T(8,128)(2,1)S(1)}, bf16[256,1280]{1,0:T(8,128)(2,1)S(1)}, u32[]{:S(2)}, u32[]{:S(2)}) collective-permute-start(bf16[256,1280]{1,0:T(8,128)(2,1)S(1)} %bitcast.259), channel_id=1, source_target_pairs={{0,8},{8,0},{1,9},{9,1},{2,10},{10,2},{3,11},{11,3},{4,12},{12,4},... | collective-permute-start | bytes 1966088 | tf_op jit(solution)/shard_map/ppermute | solution.py:121
  211.4 9.7 %collective-permute-start.8 = (bf16[256,1280]{1,0:T(8,128)(2,1)}, bf16[256,1280]{1,0:T(8,128)(2,1)}, u32[]{:S(2)}, u32[]{:S(2)}) collective-permute-start(bf16[256,1280]{1,0:T(8,128)(2,1)} %bitcast.25), channel_id=1, source_target_pairs={{0,8},{8,0},{1,9},{9,1},{2,10},{10,2},{3,11},{11,3},{4,12},{12,4},... | collective-permute-start | bytes 1966088 | tf_op jit(solution)/shard_map/ppermute | solution.py:121
  219.0 19.4 %collective-permute-start.6 = (bf16[256,1280]{1,0:T(8,128)(2,1)}, bf16[256,1280]{1,0:T(8,128)(2,1)}, u32[]{:S(2)}, u32[]{:S(2)}) collective-permute-start(bf16[256,1280]{1,0:T(8,128)(2,1)} %multiply_convert_fusion.4), channel_id=1, source_target_pairs={{0,8},{8,0},{1,9},{9,1},{2,10},{10,2},{3,11},{11,3},{4,12},{12,4},... | collective-permute-start | bytes 1966088 | tf_op jit(solution)/shard_map/ppermute | solution.py:121
  247.2 102.5 %collective-permute-start.7 = (f32[256,1280]{1,0:T(8,128)}, f32[256,1280]{1,0:T(8,128)}, u32[]{:S(2)}, u32[]{:S(2)}) collective-permute-start(f32[256,1280]{1,0:T(8,128)} %fusion.88), channel_id=1, source_target_pairs={{0,8},{8,0},{1,9},{9,1},{2,10},{10,2},{3,11},{11,3},{4,12},{12,4},... | collective-permute-start | bytes 3932168 | tf_op jit(solution)/shard_map/ppermute | solution.py:121
  250.1 85.6 %collective-permute-start.9 = (f32[256,1280]{1,0:T(8,128)}, f32[256,1280]{1,0:T(8,128)}, u32[]{:S(2)}, u32[]{:S(2)}) collective-permute-start(f32[256,1280]{1,0:T(8,128)} %convolution_add_fusion.8), channel_id=1, source_target_pairs={{0,8},{8,0},{1,9},{9,1},{2,10},{10,2},{3,11},{11,3},{4,12},{12,4},... | collective-permute-start | bytes 3932168 | tf_op jit(solution)/shard_map/ppermute | solution.py:121
  251.0 21.1 %collective-permute-start.35 = (bf16[640,640]{1,0:T(8,128)(2,1)S(1)}, bf16[640,640]{1,0:T(8,128)(2,1)S(1)}, u32[]{:S(2)}, u32[]{:S(2)}) collective-permute-start(bf16[640,640]{1,0:T(8,128)(2,1)S(1)} %convolution_convert_fusion.5), channel_id=1, source_target_pairs={{0,16},{16,0},{1,17},{17,1},{2,18},{18,2},{3,19},{19,3},{4,20},{20... | collective-permute-start | bytes 2457608 | tf_op jit(solution)/shard_map/ppermute | solution.py:121
  254.1 35.7 %collective-permute-start.36 = (bf16[640,640]{1,0:T(8,128)(2,1)}, bf16[640,640]{1,0:T(8,128)(2,1)}, u32[]{:S(2)}, u32[]{:S(2)}) collective-permute-start(bf16[640,640]{1,0:T(8,128)(2,1)} %convolution_convert_fusion.4), channel_id=1, source_target_pairs={{0,16},{16,0},{1,17},{17,1},{2,18},{18,2},{3,19},{19,3},{4,20},{20... | collective-permute-start | bytes 2457608 | tf_op jit(solution)/shard_map/ppermute | solution.py:121
  256.3 50.4 %collective-permute-start.45 = (bf16[320,1280]{1,0:T(8,128)(2,1)}, bf16[320,1280]{1,0:T(8,128)(2,1)}, u32[]{:S(2)}, u32[]{:S(2)}) collective-permute-start(bf16[320,1280]{1,0:T(8,128)(2,1)} %convolution_convert_fusion), channel_id=1, source_target_pairs={{0,16},{16,0},{1,17},{17,1},{2,18},{18,2},{3,19},{19,3},{4,20},{20... | collective-permute-start | bytes 2457608 | tf_op jit(solution)/shard_map/ppermute | solution.py:121
  308.9 8.2 %collective-permute-start.46 = (bf16[2,40,1280]{2,1,0:T(8,128)(2,1)S(1)}, bf16[2,40,1280]{2,1,0:T(8,128)(2,1)S(1)}, u32[]{:S(2)}, u32[]{:S(2)}) collective-permute-start(bf16[2,40,1280]{2,1,0:T(8,128)(2,1)S(1)} %get-tuple-element.58), channel_id=1, source_target_pairs={{0,2},{1,3},{8,10},{9,11},{16,18},{17,19},{24,26},{25,27}} | collective-permute-start | bytes 614408 | tf_op jit(solution)/shard_map/ppermute | solution.py:162
  312.7 11.7 %collective-permute-start.37 = (bf16[2,80,1280]{2,1,0:T(8,128)(2,1)S(1)}, bf16[2,80,1280]{2,1,0:T(8,128)(2,1)S(1)}, u32[]{:S(2)}, u32[]{:S(2)}) collective-permute-start(bf16[2,80,1280]{2,1,0:T(8,128)(2,1)S(1)} %get-tuple-element.51), channel_id=1, source_target_pairs={{0,2},{1,3},{8,10},{9,11},{16,18},{17,19},{24,26},{25,27}} | collective-permute-start | bytes 1228808 | tf_op jit(solution)/shard_map/ppermute | solution.py:162
  314.0 41.3 %collective-permute-start.40 = (bf16[2,80,1280]{2,1,0:T(8,128)(2,1)}, bf16[2,80,1280]{2,1,0:T(8,128)(2,1)}, u32[]{:S(2)}, u32[]{:S(2)}) collective-permute-start(bf16[2,80,1280]{2,1,0:T(8,128)(2,1)} %get-tuple-element.52), channel_id=1, source_target_pairs={{6,4},{7,5},{14,12},{15,13},{22,20},{23,21},{30,28},{31,29}} | collective-permute-start | bytes 1228808 | tf_op jit(solution)/shard_map/ppermute | solution.py:165
  317.0 12.6 %collective-permute-start.49 = (bf16[2,40,1280]{2,1,0:T(8,128)(2,1)S(1)}, bf16[2,40,1280]{2,1,0:T(8,128)(2,1)S(1)}, u32[]{:S(2)}, u32[]{:S(2)}) collective-permute-start(bf16[2,40,1280]{2,1,0:T(8,128)(2,1)S(1)} %get-tuple-element.59), channel_id=1, source_target_pairs={{6,4},{7,5},{14,12},{15,13},{22,20},{23,21},{30,28},{31,29}} | collective-permute-start | bytes 614408 | tf_op jit(solution)/shard_map/ppermute | solution.py:165
  324.3 9.2 %collective-permute-start.47 = (bf16[2,40,1280]{2,1,0:T(8,128)(2,1)S(1)}, bf16[2,40,1280]{2,1,0:T(8,128)(2,1)S(1)}, u32[]{:S(2)}, u32[]{:S(2)}) collective-permute-start(bf16[2,40,1280]{2,1,0:T(8,128)(2,1)S(1)} %fusion.55), channel_id=1, source_target_pairs={{0,2},{2,4},{1,3},{3,5},{8,10},{10,12},{9,11},{11,13},{16,18},{18,... | collective-permute-start | bytes 614408 | tf_op jit(solution)/shard_map/ppermute | solution.py:162
  329.6 25.7 %collective-permute-start.38 = (bf16[2,80,1280]{2,1,0:T(8,128)(2,1)}, bf16[2,80,1280]{2,1,0:T(8,128)(2,1)}, u32[]{:S(2)}, u32[]{:S(2)}) collective-permute-start(bf16[2,80,1280]{2,1,0:T(8,128)(2,1)} %fusion.37), channel_id=1, source_target_pairs={{0,2},{2,4},{1,3},{3,5},{8,10},{10,12},{9,11},{11,13},{16,18},{18,... | collective-permute-start | bytes 1228808 | tf_op jit(solution)/shard_map/ppermute | solution.py:162
  334.4 18.6 %collective-permute-start.50 = (bf16[2,40,1280]{2,1,0:T(8,128)(2,1)}, bf16[2,40,1280]{2,1,0:T(8,128)(2,1)}, u32[]{:S(2)}, u32[]{:S(2)}) collective-permute-start(bf16[2,40,1280]{2,1,0:T(8,128)(2,1)} %get-tuple-element.57), channel_id=1, source_target_pairs={{4,2},{6,4},{5,3},{7,5},{12,10},{14,12},{13,11},{15,13},{20,18},{2... | collective-permute-start | bytes 614408 | tf_op jit(solution)/shard_map/ppermute | solution.py:165
  335.8 28.7 %collective-permute-start.48 = (bf16[2,40,1280]{2,1,0:T(8,128)(2,1)}, bf16[2,40,1280]{2,1,0:T(8,128)(2,1)}, u32[]{:S(2)}, u32[]{:S(2)}) collective-permute-start(bf16[2,40,1280]{2,1,0:T(8,128)(2,1)} %get-tuple-element.56), channel_id=1, source_target_pairs={{0,2},{2,4},{4,6},{1,3},{3,5},{5,7},{8,10},{10,12},{12,14},{9,11},... | collective-permute-start | bytes 614408 | tf_op jit(solution)/shard_map/ppermute | solution.py:162
  349.7 18.0 %collective-permute-start.10 = (bf16[256,1280]{1,0:T(8,128)(2,1)S(1)}, bf16[256,1280]{1,0:T(8,128)(2,1)S(1)}, u32[]{:S(2)}, u32[]{:S(2)}) collective-permute-start(bf16[256,1280]{1,0:T(8,128)(2,1)S(1)} %get-tuple-element.36), channel_id=1, source_target_pairs={{0,8},{8,0},{1,9},{9,1},{2,10},{10,2},{3,11},{11,3},{4,12},{12,4},... | collective-permute-start | bytes 1966088 | tf_op jit(solution)/shard_map/ppermute | solution.py:121
  354.0 10.5 %collective-permute-start.51 = (bf16[2,40,1280]{2,1,0:T(8,128)(2,1)S(1)}, bf16[2,40,1280]{2,1,0:T(8,128)(2,1)S(1)}, u32[]{:S(2)}, u32[]{:S(2)}) collective-permute-start(bf16[2,40,1280]{2,1,0:T(8,128)(2,1)S(1)} %fusion.54), channel_id=1, source_target_pairs={{2,0},{4,2},{6,4},{3,1},{5,3},{7,5},{10,8},{12,10},{14,12},{11,9},... | collective-permute-start | bytes 614408 | tf_op jit(solution)/shard_map/ppermute | solution.py:165
  357.7 54.8 %collective-permute-start.41 = (bf16[2,80,1280]{2,1,0:T(8,128)(2,1)}, bf16[2,80,1280]{2,1,0:T(8,128)(2,1)}, u32[]{:S(2)}, u32[]{:S(2)}) collective-permute-start(bf16[2,80,1280]{2,1,0:T(8,128)(2,1)} %get-tuple-element.50), channel_id=1, source_target_pairs={{4,2},{6,4},{5,3},{7,5},{12,10},{14,12},{13,11},{15,13},{20,18},{2... | collective-permute-start | bytes 1228808 | tf_op jit(solution)/shard_map/ppermute | solution.py:165
  359.1 58.8 %collective-permute-start.39 = (bf16[2,80,1280]{2,1,0:T(8,128)(2,1)}, bf16[2,80,1280]{2,1,0:T(8,128)(2,1)}, u32[]{:S(2)}, u32[]{:S(2)}) collective-permute-start(bf16[2,80,1280]{2,1,0:T(8,128)(2,1)} %get-tuple-element.49), channel_id=1, source_target_pairs={{0,2},{2,4},{4,6},{1,3},{3,5},{5,7},{8,10},{10,12},{12,14},{9,11},... | collective-permute-start | bytes 1228808 | tf_op jit(solution)/shard_map/ppermute | solution.py:162
  366.3 178.7 %collective-permute-start.52 = (bf16[40,1280]{1,0:T(8,128)(2,1)}, bf16[40,1280]{1,0:T(8,128)(2,1)}, u32[]{:S(2)}, u32[]{:S(2)}) collective-permute-start(bf16[40,1280]{1,0:T(8,128)(2,1)} %fusion.104), channel_id=1, source_target_pairs={{0,1},{1,0},{2,3},{3,2},{4,5},{5,4},{6,7},{7,6},{8,9},{9,8},{10,11... | collective-permute-start | bytes 307208 | tf_op jit(solution)/shard_map/ppermute | solution.py:121
  402.8 71.1 %collective-permute-start.11 = (f32[256,1280]{1,0:T(8,128)}, f32[256,1280]{1,0:T(8,128)}, u32[]{:S(2)}, u32[]{:S(2)}) collective-permute-start(f32[256,1280]{1,0:T(8,128)} %convolution_add_fusion.6), channel_id=1, source_target_pairs={{0,8},{8,0},{1,9},{9,1},{2,10},{10,2},{3,11},{11,3},{4,12},{12,4},... | collective-permute-start | bytes 3932168 | tf_op jit(solution)/shard_map/ppermute | solution.py:121
  408.0 112.6 %collective-permute-start.13 = (f32[256,1280]{1,0:T(8,128)}, f32[256,1280]{1,0:T(8,128)}, u32[]{:S(2)}, u32[]{:S(2)}) collective-permute-start(f32[256,1280]{1,0:T(8,128)} %convolution_add_fusion.2), channel_id=1, source_target_pairs={{0,8},{8,0},{1,9},{9,1},{2,10},{10,2},{3,11},{11,3},{4,12},{12,4},... | collective-permute-start | bytes 3932168 | tf_op jit(solution)/shard_map/ppermute | solution.py:121
  413.8 13.4 %collective-permute-start.42 = (bf16[2,80,1280]{2,1,0:T(8,128)(2,1)S(1)}, bf16[2,80,1280]{2,1,0:T(8,128)(2,1)S(1)}, u32[]{:S(2)}, u32[]{:S(2)}) collective-permute-start(bf16[2,80,1280]{2,1,0:T(8,128)(2,1)S(1)} %fusion.36), channel_id=1, source_target_pairs={{2,0},{4,2},{6,4},{3,1},{5,3},{7,5},{10,8},{12,10},{14,12},{11,9},... | collective-permute-start | bytes 1228808 | tf_op jit(solution)/shard_map/ppermute | solution.py:165
  429.7 21.6 %collective-permute-start.16 = (bf16[640,640]{1,0:T(8,128)(2,1)}, bf16[640,640]{1,0:T(8,128)(2,1)}, u32[]{:S(2)}, u32[]{:S(2)}) collective-permute-start(bf16[640,640]{1,0:T(8,128)(2,1)} %convolution_convert_fusion.6), channel_id=1, source_target_pairs={{0,16},{16,0},{1,17},{17,1},{2,18},{18,2},{3,19},{19,3},{4,20},{20... | collective-permute-start | bytes 2457608 | tf_op jit(solution)/shard_map/ppermute | solution.py:121
  435.7 33.2 %collective-permute-start.15 = (bf16[640,640]{1,0:T(8,128)(2,1)}, bf16[640,640]{1,0:T(8,128)(2,1)}, u32[]{:S(2)}, u32[]{:S(2)}) collective-permute-start(bf16[640,640]{1,0:T(8,128)(2,1)} %convolution_convert_fusion.7), channel_id=1, source_target_pairs={{0,16},{16,0},{1,17},{17,1},{2,18},{18,2},{3,19},{19,3},{4,20},{20... | collective-permute-start | bytes 2457608 | tf_op jit(solution)/shard_map/ppermute | solution.py:121
  451.3 35.0 %collective-permute-start.14 = (bf16[640,640]{1,0:T(8,128)(2,1)}, bf16[640,640]{1,0:T(8,128)(2,1)S(1)}, u32[]{:S(2)}, u32[]{:S(2)}) collective-permute-start(bf16[640,640]{1,0:T(8,128)(2,1)} %convolution_convert_fusion.8), channel_id=1, source_target_pairs={{0,16},{16,0},{1,17},{17,1},{2,18},{18,2},{3,19},{19,3},{4,20},{20... | collective-permute-start | bytes 2457608 | tf_op jit(solution)/shard_map/ppermute | solution.py:121
  468.9 41.3 %collective-permute-start.27 = (bf16[320,1280]{1,0:T(8,128)(2,1)}, bf16[320,1280]{1,0:T(8,128)(2,1)}, u32[]{:S(2)}, u32[]{:S(2)}) collective-permute-start(bf16[320,1280]{1,0:T(8,128)(2,1)} %convolution_convert_fusion.1), channel_id=1, source_target_pairs={{0,16},{16,0},{1,17},{17,1},{2,18},{18,2},{3,19},{19,3},{4,20},{20... | collective-permute-start | bytes 2457608 | tf_op jit(solution)/shard_map/ppermute | solution.py:121
  473.9 72.9 %collective-permute-start.44 = (f32[80,640]{1,0:T(8,128)}, f32[80,640]{1,0:T(8,128)S(1)}, u32[]{:S(2)}, u32[]{:S(2)}) collective-permute-start(f32[80,640]{1,0:T(8,128)} %bitcast.245), channel_id=1, source_target_pairs={{0,8},{8,0},{1,9},{9,1},{2,10},{10,2},{3,11},{11,3},{4,12},{12,4},... | collective-permute-start | bytes 614408 | tf_op jit(solution)/shard_map/ppermute | solution.py:121
  486.3 35.6 %collective-permute-start.12 = (bf16[256,1280]{1,0:T(8,128)(2,1)}, bf16[256,1280]{1,0:T(8,128)(2,1)}, u32[]{:S(2)}, u32[]{:S(2)}) collective-permute-start(bf16[256,1280]{1,0:T(8,128)(2,1)} %fusion.9), channel_id=1, source_target_pairs={{16,0},{17,1},{18,2},{19,3},{20,4},{21,5},{22,6},{23,7},{24,8},{25... | collective-permute-start | bytes 1966088 | tf_op jit(solution)/shard_map/ppermute | solution.py:335
  515.3 14.0 %collective-permute-start.28 = (bf16[2,40,1280]{2,1,0:T(8,128)(2,1)}, bf16[2,40,1280]{2,1,0:T(8,128)(2,1)}, u32[]{:S(2)}, u32[]{:S(2)}) collective-permute-start(bf16[2,40,1280]{2,1,0:T(8,128)(2,1)} %get-tuple-element.62), channel_id=1, source_target_pairs={{0,2},{1,3},{8,10},{9,11},{16,18},{17,19},{24,26},{25,27}} | collective-permute-start | bytes 614408 | tf_op jit(solution)/shard_map/ppermute | solution.py:162
  520.6 26.7 %collective-permute-start.31 = (bf16[2,40,1280]{2,1,0:T(8,128)(2,1)}, bf16[2,40,1280]{2,1,0:T(8,128)(2,1)}, u32[]{:S(2)}, u32[]{:S(2)}) collective-permute-start(bf16[2,40,1280]{2,1,0:T(8,128)(2,1)} %get-tuple-element.63), channel_id=1, source_target_pairs={{6,4},{7,5},{14,12},{15,13},{22,20},{23,21},{30,28},{31,29}} | collective-permute-start | bytes 614408 | tf_op jit(solution)/shard_map/ppermute | solution.py:165
  525.8 7.4 %collective-permute-start.17 = (f32[4,2,1,2,120]{4,3,1,0,2:T(2,128)S(1)}, f32[4,2,1,2,120]{4,3,1,0,2:T(2,128)S(1)}, u32[]{:S(2)}, u32[]{:S(2)}) collective-permute-start(f32[4,2,1,2,120]{4,3,1,0,2:T(2,128)S(1)} %select_n.442), channel_id=1, source_target_pairs={{0,16},{16,0},{1,17},{17,1},{2,18},{18,2},{3,19},{19,3},{4,20},{20... | collective-permute-start | bytes 23048 | tf_op jit(solution)/shard_map/ppermute | solution.py:121
  531.1 16.2 %collective-permute-start.29 = (bf16[2,40,1280]{2,1,0:T(8,128)(2,1)}, bf16[2,40,1280]{2,1,0:T(8,128)(2,1)}, u32[]{:S(2)}, u32[]{:S(2)}) collective-permute-start(bf16[2,40,1280]{2,1,0:T(8,128)(2,1)} %fusion.60), channel_id=1, source_target_pairs={{0,2},{2,4},{1,3},{3,5},{8,10},{10,12},{9,11},{11,13},{16,18},{18,... | collective-permute-start | bytes 614408 | tf_op jit(solution)/shard_map/ppermute | solution.py:162
  541.5 11.9 %collective-permute-start.18 = (bf16[2,128,1280]{2,1,0:T(8,128)(2,1)}, bf16[2,128,1280]{2,1,0:T(8,128)(2,1)}, u32[]{:S(2)}, u32[]{:S(2)}) collective-permute-start(bf16[2,128,1280]{2,1,0:T(8,128)(2,1)} %get-tuple-element.44), channel_id=1, source_target_pairs={{0,2},{1,3},{8,10},{9,11},{16,18},{17,19},{24,26},{25,27}} | collective-permute-start | bytes 1966088 | tf_op jit(solution)/shard_map/ppermute | solution.py:162
  549.2 15.3 %collective-permute-start.32 = (bf16[2,40,1280]{2,1,0:T(8,128)(2,1)}, bf16[2,40,1280]{2,1,0:T(8,128)(2,1)}, u32[]{:S(2)}, u32[]{:S(2)}) collective-permute-start(bf16[2,40,1280]{2,1,0:T(8,128)(2,1)} %get-tuple-element.61), channel_id=1, source_target_pairs={{4,2},{6,4},{5,3},{7,5},{12,10},{14,12},{13,11},{15,13},{20,18},{2... | collective-permute-start | bytes 614408 | tf_op jit(solution)/shard_map/ppermute | solution.py:165
  550.5 16.3 %collective-permute-start.21 = (bf16[2,128,1280]{2,1,0:T(8,128)(2,1)S(1)}, bf16[2,128,1280]{2,1,0:T(8,128)(2,1)}, u32[]{:S(2)}, u32[]{:S(2)}) collective-permute-start(bf16[2,128,1280]{2,1,0:T(8,128)(2,1)S(1)} %copy-done.62), channel_id=1, source_target_pairs={{6,4},{7,5},{14,12},{15,13},{22,20},{23,21},{30,28},{31,29}} | collective-permute-start | bytes 1966088 | tf_op jit(solution)/shard_map/ppermute | solution.py:165
  555.8 15.1 %collective-permute-start.19 = (bf16[2,128,1280]{2,1,0:T(8,128)(2,1)}, bf16[2,128,1280]{2,1,0:T(8,128)(2,1)}, u32[]{:S(2)}, u32[]{:S(2)}) collective-permute-start(bf16[2,128,1280]{2,1,0:T(8,128)(2,1)} %fusion.22), channel_id=1, source_target_pairs={{0,2},{2,4},{1,3},{3,5},{8,10},{10,12},{9,11},{11,13},{16,18},{18,... | collective-permute-start | bytes 1966088 | tf_op jit(solution)/shard_map/ppermute | solution.py:162
  563.2 10.7 %collective-permute-start.30 = (bf16[2,40,1280]{2,1,0:T(8,128)(2,1)}, bf16[2,40,1280]{2,1,0:T(8,128)(2,1)S(1)}, u32[]{:S(2)}, u32[]{:S(2)}) collective-permute-start(bf16[2,40,1280]{2,1,0:T(8,128)(2,1)} %get-tuple-element.60), channel_id=1, source_target_pairs={{0,2},{2,4},{4,6},{1,3},{3,5},{5,7},{8,10},{10,12},{12,14},{9,11},... | collective-permute-start | bytes 614408 | tf_op jit(solution)/shard_map/ppermute | solution.py:162
  565.5 8.4 %collective-permute-start.33 = (bf16[2,40,1280]{2,1,0:T(8,128)(2,1)S(1)}, bf16[2,40,1280]{2,1,0:T(8,128)(2,1)S(1)}, u32[]{:S(2)}, u32[]{:S(2)}) collective-permute-start(bf16[2,40,1280]{2,1,0:T(8,128)(2,1)S(1)} %fusion.59), channel_id=1, source_target_pairs={{2,0},{4,2},{6,4},{3,1},{5,3},{7,5},{10,8},{12,10},{14,12},{11,9},... | collective-permute-start | bytes 614408 | tf_op jit(solution)/shard_map/ppermute | solution.py:165
  573.2 7.6 %collective-permute-start.22 = (bf16[2,128,1280]{2,1,0:T(8,128)(2,1)S(1)}, bf16[2,128,1280]{2,1,0:T(8,128)(2,1)S(1)}, u32[]{:S(2)}, u32[]{:S(2)}) collective-permute-start(bf16[2,128,1280]{2,1,0:T(8,128)(2,1)S(1)} %get-tuple-element.43), channel_id=1, source_target_pairs={{4,2},{6,4},{5,3},{7,5},{12,10},{14,12},{13,11},{15,13},{20,18},{2... | collective-permute-start | bytes 1966088 | tf_op jit(solution)/shard_map/ppermute | solution.py:165
  574.0 9.6 %collective-permute-start.34 = (bf16[40,1280]{1,0:T(8,128)(2,1)S(1)}, bf16[40,1280]{1,0:T(8,128)(2,1)S(1)}, u32[]{:S(2)}, u32[]{:S(2)}) collective-permute-start(bf16[40,1280]{1,0:T(8,128)(2,1)S(1)} %fusion.103), channel_id=1, source_target_pairs={{0,1},{1,0},{2,3},{3,2},{4,5},{5,4},{6,7},{7,6},{8,9},{9,8},{10,11... | collective-permute-start | bytes 307208 | tf_op jit(solution)/shard_map/ppermute | solution.py:121
  576.5 12.4 %collective-permute-start.20 = (bf16[2,128,1280]{2,1,0:T(8,128)(2,1)S(1)}, bf16[2,128,1280]{2,1,0:T(8,128)(2,1)S(1)}, u32[]{:S(2)}, u32[]{:S(2)}) collective-permute-start(bf16[2,128,1280]{2,1,0:T(8,128)(2,1)S(1)} %get-tuple-element.42), channel_id=1, source_target_pairs={{0,2},{2,4},{4,6},{1,3},{3,5},{5,7},{8,10},{10,12},{12,14},{9,11},... | collective-permute-start | bytes 1966088 | tf_op jit(solution)/shard_map/ppermute | solution.py:162
  582.3 20.1 %collective-permute-start.23 = (bf16[2,128,1280]{2,1,0:T(8,128)(2,1)S(1)}, bf16[2,128,1280]{2,1,0:T(8,128)(2,1)S(1)}, u32[]{:S(2)}, u32[]{:S(2)}) collective-permute-start(bf16[2,128,1280]{2,1,0:T(8,128)(2,1)S(1)} %fusion.21), channel_id=1, source_target_pairs={{2,0},{4,2},{6,4},{3,1},{5,3},{7,5},{10,8},{12,10},{14,12},{11,9},... | collective-permute-start | bytes 1966088 | tf_op jit(solution)/shard_map/ppermute | solution.py:165
  604.2 7.1 %collective-permute-start.24 = (bf16[128,1280]{1,0:T(8,128)(2,1)S(1)}, bf16[128,1280]{1,0:T(8,128)(2,1)S(1)}, u32[]{:S(2)}, u32[]{:S(2)}) collective-permute-start(bf16[128,1280]{1,0:T(8,128)(2,1)S(1)} %fusion.67), channel_id=1, source_target_pairs={{0,1},{1,0},{2,3},{3,2},{4,5},{5,4},{6,7},{7,6},{8,9},{9,8},{10,11... | collective-permute-start | bytes 983048 | tf_op jit(solution)/shard_map/ppermute | solution.py:121
  (90 other events, 735.5 us)
Sparse Core Ops, SparseCore 0:
  15.1 89.4 all-gather.3
  107.9 95.2 all-gather.5
